TPU v7x, 32 devices: a whole 2x2x4 slice. The times are simulated.
32 devices in a mesh: groups: 2 (over y), section: 2 (over core), ep: 4 (over z), tp: 2 (over x).
Axes of the slice: x: 2, y: 2, z: 4, core: 2. Of those that a mesh axis runs over, the one named last changes fastest.
Arguments:
- tokens: bfloat16 [16384, 6144], P(('groups', 'section', 'ep'), 'tp'), parts along dimension 0, may hold values from -6 to 6
- w_kv: bfloat16 [6144, 2048], P(('section', 'ep'), 'tp'), may hold values from -0.078125 to 0.078125
- page_target: int32 [1024, 1], P(('groups', 'section', 'ep')), parts along dimension 0, may hold values from 0 to 7; in each aligned block of 64 rows (0 to 63, 64 to 127, ...) at most 16 rows name the same one
- queries: bfloat16 [256, 2, 6144], P(('groups', 'section', 'ep'), None, 'tp'), parts along dimension 0, may hold values from -110 to 110
- decoded_keys: bfloat16 [256, 2, 1024], P(('groups', 'section', 'ep'), None, 'tp'), parts along dimension 0, may hold values from -4 to 4
- decoded_values: bfloat16 [256, 2, 1024], P(('groups', 'section', 'ep'), None, 'tp'), parts along dimension 0, may hold values from -6 to 6
Outputs:
- attended: bfloat16 [256, 2, 6144], P(('groups', 'section', 'ep'), None, 'tp'), parts along dimension 0
There are 2 independent parts, one for each index of `groups`. A program takes and returns all parts, laid end to end along the dimension named above; an argument that names none is the same for every part. Nothing has to cross between parts.
Inputs may be any that keep to these rules, and one draw needn't show every extreme that they name: `page_target`: every request owns at least one page; request r is decoded by the forks 16 * r to 16 * r + 15; among the 64 pages of one device at most 16 belong to one request, and in every draw some device holds exactly 16 pages of one request.
All inputs are finite; a program needn't handle non-finite values.
Results may differ from a plain program's by a relative error of at most 0.0077.
Values may be sent and summed in bfloat16 or wider, within the bound.
A program may use at most 128 MiB of HBM per device.

v0:
```python
import math

import jax
import jax.numpy as jnp
from jax import lax
from jax.sharding import PartitionSpec as P

QUERY_HEADS = 48
KEY_VALUE_HEADS = 8
HEAD_SIZE = 128
PAGE = 16


def local(tokens, w_kv, page_target, queries, decoded_keys, decoded_values):
    gathered = lax.all_gather(tokens, "tp", axis=1, tiled=True)
    kv_width = w_kv.shape[1]
    projected_rows = jnp.dot(
        gathered,
        lax.all_gather(w_kv, ("section", "ep"), axis=0, tiled=True),
        preferred_element_type=jnp.float32,
    )
    page_rows = gathered.shape[0] // PAGE
    page_data = projected_rows.astype(jnp.bfloat16).reshape(page_rows, PAGE * kv_width)
    targets = page_target[:, 0]
    dest_count = lax.axis_size(("section", "ep"))
    capacity = max(2, 2 * page_rows // dest_count)
    same_target = targets[:, None] == targets[None, :]
    earlier = jnp.arange(page_rows)[None, :] < jnp.arange(page_rows)[:, None]
    ranks = jnp.sum((same_target & earlier).astype(jnp.int32), axis=1)
    slot_index = targets * capacity + ranks
    placed = slot_index[None, :] == jnp.arange(dest_count * capacity, dtype=jnp.int32)[:, None]
    outgoing = jnp.dot(
        placed.astype(jnp.bfloat16), page_data, preferred_element_type=jnp.float32
    ).astype(jnp.bfloat16)
    filled = jnp.sum(placed.astype(jnp.int32), axis=1)
    arrived, live_slots = (
        lax.all_to_all(
            outgoing.reshape(dest_count, capacity, PAGE, kv_width),
            ("section", "ep"),
            split_axis=0,
            concat_axis=0,
            tiled=True,
        ),
        lax.all_to_all(
            filled.reshape(dest_count, capacity),
            ("section", "ep"),
            split_axis=0,
            concat_axis=0,
            tiled=True,
        ),
    )
    head_pairs = kv_width // (2 * HEAD_SIZE)
    arrived = arrived.reshape(-1, head_pairs, 2, HEAD_SIZE)
    prompt_keys = arrived[:, :, 0]
    prompt_values = arrived[:, :, 1]
    slot_live = jnp.repeat(live_slots.reshape(-1), PAGE) > 0
    forks = queries.shape[0]
    steps = queries.shape[1]
    grouped_heads = QUERY_HEADS // KEY_VALUE_HEADS
    query_head_list = queries.reshape(forks, steps, head_pairs, grouped_heads, HEAD_SIZE)
    latest_keys = decoded_keys.reshape(forks, steps, head_pairs, HEAD_SIZE)
    latest_values = decoded_values.reshape(forks, steps, head_pairs, HEAD_SIZE)
    inv_root = 1.0 / math.sqrt(HEAD_SIZE)
    prompt_scores = (
        jnp.einsum(
            "fsgjd,tgd->gfsjt", query_head_list, prompt_keys, preferred_element_type=jnp.float32
        )
        * inv_root
    )
    prompt_scores = jnp.where(slot_live, prompt_scores, -jnp.inf)
    fresh_scores = (
        jnp.einsum(
            "fsgjd,fugd->gfsju", query_head_list, latest_keys, preferred_element_type=jnp.float32
        )
        * inv_root
    )
    causal = jnp.arange(steps)[None, :] <= jnp.arange(steps)[:, None]
    fresh_scores = jnp.where(causal[None, None, :, None, :], fresh_scores, -jnp.inf)
    peak_score = jnp.maximum(jnp.max(prompt_scores, -1), jnp.max(fresh_scores, -1))[..., None]
    prompt_exp = jnp.exp(prompt_scores - peak_score)
    fresh_exp = jnp.exp(fresh_scores - peak_score)
    normalizer = jnp.sum(prompt_exp, -1, keepdims=True) + jnp.sum(fresh_exp, -1, keepdims=True)
    prompt_weights = (prompt_exp / normalizer).astype(jnp.bfloat16)
    fresh_weights = (fresh_exp / normalizer).astype(jnp.bfloat16)
    combined = jnp.einsum(
        "gfsjt,tgd->fsgjd", prompt_weights, prompt_values, preferred_element_type=jnp.float32
    )
    combined = combined + jnp.einsum(
        "gfsju,fugd->fsgjd", fresh_weights, latest_values, preferred_element_type=jnp.float32
    )
    return combined.reshape(forks, steps, -1).astype(jnp.bfloat16)


def solution(mesh):
    in_specs = (
        P(("groups", "section", "ep"), "tp"),
        P(("section", "ep"), "tp"),
        P(("groups", "section", "ep"), None),
        P(("groups", "section", "ep"), None, "tp"),
        P(("groups", "section", "ep"), None, "tp"),
        P(("groups", "section", "ep"), None, "tp"),
    )
    out_specs = P(("groups", "section", "ep"), None, "tp")
    return jax.shard_map(local, mesh=mesh, in_specs=in_specs, out_specs=out_specs, check_vma=False)
```

profile of v0, /device:TPU:0, one launch (start us, length us, event | category | flops | bytes accessed | tf_op | source)
XLA Modules:
  0.0 448.5 jit_solution(13666642208545657479)
XLA Ops:
  6.5 0.7 all-gather.3.cloned.1.call-update
  7.3 0.7 all-gather.5.cloned.1.call-update
  8.0 0.2 convert_reduce_fusion.1
  8.3 0.7 all_to_all.10
  9.0 6.3 %all-to-all-start.1 = ((s32[8,1,16]{2,1,0:T(1,128)}), s32[8,1,16]{2,1,0:T(1,128)S(1)}, u32[]{:S(2)}, u32[]{:S(2)}) async-start(s32[8,1,16]{2,1,0:T(1,128)} %bitcast.4), calls=%async_computation.1 | async-start | bytes 8192 | tf_op jit(solution)/shard_map/all_to_all | solution.py:44
  15.3 148.8 %all-gather.3.cloned.1.call-done = bf16[1024,6144]{1,0:T(8,128)(2,1)} async-done(((bf16[1024,3072]{1,0:T(8,128)(2,1)}), bf16[1024,6144]{1,0:T(8,128)(2,1)}) %all-gather.3.cloned.1.call-update) | async-done | bytes 12582928 | tf_op jit(solution)/shard_map/all_gather | solution.py:15
  164.1 118.4 %all-gather.5.cloned.1.call-done = bf16[6144,1024]{1,0:T(8,128)(2,1)} async-done(((bf16[768,1024]{1,0:T(8,128)(2,1)}), bf16[6144,1024]{1,0:T(8,128)(2,1)}) %all-gather.5.cloned.1.call-update) | async-done | bytes 12582928 | tf_op jit(solution)/shard_map/all_gather | solution.py:19
  282.5 18.8 %convolution_convert_fusion.1 = bf16[1024,1024]{1,0:T(8,128)(2,1)} fusion(bf16[1024,6144]{1,0:T(8,128)(2,1)} %all-gather.3.cloned.1.call-done, bf16[6144,1024]{1,0:T(8,128)(2,1)} %all-gather.5.cloned.1.call-done), kind=kOutput, calls=%fused_computation.11 | convolution fusion | flops 12885950464 | bytes 27262976 | tf_op jit(solution)/shard_map/dot_general | solution.py:17
  301.3 2.9 reshape.63
  304.2 1.4 convolution_convert_fusion
  305.5 4.7 %copy.98 = bf16[16,8,16,1024]{3,2,1,0:T(8,128)(2,1)} copy(bf16[16,8,16,1024]{3,1,2,0:T(8,128)(2,1)S(1)} %bitcast.68) | data formatting | bytes 8388608
  310.2 4.9 %all-to-all-start = ((bf16[8,16,16,1024]{3,2,1,0:T(8,128)(2,1)}), bf16[8,16,16,1024]{3,2,1,0:T(8,128)(2,1)}, u32[]{:S(2)}, u32[]{:S(2)}) async-start(bf16[8,16,16,1024]{3,2,1,0:T(8,128)(2,1)} %bitcast.67), calls=%async_computation | async-start | bytes 8388608 | tf_op jit(solution)/shard_map/all_to_all | solution.py:37
  315.2 0.3 reshape.66
  315.5 1.3 fusion.20
  317.2 91.3 %all-to-all-done = bf16[8,16,16,1024]{3,2,1,0:T(8,128)(2,1)} async-done(((bf16[8,16,16,1024]{3,2,1,0:T(8,128)(2,1)}), bf16[8,16,16,1024]{3,2,1,0:T(8,128)(2,1)}, u32[]{:S(2)}, u32[]{:S(2)}) %all-to-all-start) | async-done | bytes 4194336 | tf_op jit(solution)/shard_map/all_to_all | solution.py:37
  408.5 7.7 %reshape.65 = bf16[2048,4,2,128]{3,2,1,0:T(2,128)(2,1)} reshape(bf16[8,16,16,1024]{3,2,1,0:T(8,128)(2,1)} %all-to-all-done) | data formatting | bytes 8388608 | tf_op jit(solution)/shard_map/reshape | solution.py:53
  416.2 9.6 %fusion.19 = (bf16[2048,4,1,128]{3,2,1,0:T(2,128)(2,1)}, bf16[2048,4,1,128]{3,2,1,0:T(2,128)(2,1)S(1)}) fusion(bf16[2048,4,2,128]{3,2,1,0:T(2,128)(2,1)} %reshape.65), kind=kLoop, calls=%fused_computation.37 | loop fusion | bytes 8388608 | tf_op jit(solution)/shard_map/slice | solution.py:55
  425.8 3.8 bitcast_reduce_fusion
  429.6 0.1 copy.80
  429.8 4.1 fusion.1
  433.9 0.3 fusion.10
  434.4 0.3 fusion.11
  434.8 5.9 %fusion.6 = bf16[16,2,4,6,128]{4,0,3,1,2:T(8,128)(2,1)S(1)} fusion(f32[4,2048,16,2,6]{1,2,4,3,0:T(8,128)} %get-tuple-element.8, f32[4,16,2,6]{1,3,2,0:T(8,128)S(1)} %add.19, f32[4,16,2,6]{1,3,2,0:T(8,128)S(1)} %max.7, pred[2048]{0:T(1024)(128)(4,1)S(1)} %gt.16, bf16[2048,4,1,128]{3,2,1,0:T(2,128)(2,1)} %get-tuple-element.5, ...), kind=kOutput, calls=%fused_computation.14 | convolution fusion | flops 410714112 | bytes 8986624 | tf_op jit(solution)/shard_map/gfsjt,tgd->fsgjd/dot_general | solution.py:85
  440.8 0.8 reshape.73
  (26 shorter events, 1.0 us)
Async XLA Ops:
  6.5 427.9 %copy-start = (bf16[16,2,512]{2,1,0:T(2,128)(2,1)S(1)}, bf16[16,2,512]{2,1,0:T(2,128)(2,1)}, u32[]{:S(2)}) copy-start(bf16[16,2,512]{2,1,0:T(2,128)(2,1)} %param.11) | copy-start | bytes 98308
  6.5 1.5 copy-start.3
  6.5 157.6 %all-gather.3.cloned.1.call-start = ((), (), s32[]{:S(2)}) async-start(), calls=%async_computation.2 | async-start | bytes 18874368 | tf_op jit(solution)/shard_map/all_gather | solution.py:15
  7.3 275.3 %all-gather.5.cloned.1.call-start = ((), (), s32[]{:S(2)}) async-start(), calls=%async_computation.3 | async-start | bytes 14155776 | tf_op jit(solution)/shard_map/all_gather | solution.py:19
  9.0 301.3 %all-to-all-start.1 = ((s32[8,1,16]{2,1,0:T(1,128)}), s32[8,1,16]{2,1,0:T(1,128)S(1)}, u32[]{:S(2)}, u32[]{:S(2)}) async-start(s32[8,1,16]{2,1,0:T(1,128)} %bitcast.4), calls=%async_computation.1 | async-start | bytes 8192 | tf_op jit(solution)/shard_map/all_to_all | solution.py:44
  310.2 4.9 %copy-start.2 = (bf16[16,2,512]{2,1,0:T(2,128)(2,1)S(1)}, bf16[16,2,512]{2,1,0:T(2,128)(2,1)}, u32[]{:S(2)}) copy-start(bf16[16,2,512]{2,1,0:T(2,128)(2,1)} %param.10) | copy-start | bytes 98308
  310.2 4.9 %copy-start.1 = (bf16[16,2,3072]{2,1,0:T(2,128)(2,1)S(1)}, bf16[16,2,3072]{2,1,0:T(2,128)(2,1)}, u32[]{:S(2)}) copy-start(bf16[16,2,3072]{2,1,0:T(2,128)(2,1)} %param.9) | copy-start | bytes 589828
  310.2 98.2 %all-to-all-start = ((bf16[8,16,16,1024]{3,2,1,0:T(8,128)(2,1)}), bf16[8,16,16,1024]{3,2,1,0:T(8,128)(2,1)}, u32[]{:S(2)}, u32[]{:S(2)}) async-start(bf16[8,16,16,1024]{3,2,1,0:T(8,128)(2,1)} %bitcast.67), calls=%async_computation | async-start | bytes 8388608 | tf_op jit(solution)/shard_map/all_to_all | solution.py:37
Sparse Core Ops, SparseCore 0:
  8.9 155.1 all-gather.2
  165.7 116.7 all-gather.4
where the time goes:
time: 449 us; the launch traced here: 448 us
  waiting for transfers between devices  360 us (80%)
  matrix products  31.5 us (7%)
  local copies, waits for them, and re-layouts  27.6 us (6%)
  between operations  13.5 us (3%)
  starting transfers between devices  11.2 us (2%)
  other arithmetic  4.73 us (1%)
    all_gather x1, waiting for transfers between devices, local(): gathered = lax.all_gather(tokens, 'tp', axis=1, tiled=True)  149 us
    all_gather x1, waiting for transfers between devices, local(): lax.all_gather(w_kv, ('section', 'ep'), axis=0, tiled=True)  118 us
    all_to_all x1, waiting for transfers between devices, local(): lax.all_to_all(outgoing.reshape(dest_count, capacity, PAGE, kv_width), ('...  91.3 us
    dot_general x1, matrix products, local(): jnp.dot(gathered, lax.all_gather(w_kv, ('section', 'ep'), axis=0, tiled=T...  18.8 us
    slice x1, local copies, waits for them, and re-layouts, local(): prompt_values = arrived[:, :, 1]  9.63 us
  transfers between devices with their start and end apart: 4, of which 3 were waited for; matrix products, arithmetic and copies ran while one was open for 7% of the time, Pallas kernels for 0%

commit v1 on v0

--- a/solution.py
+++ b/solution.py
@@ -1,25 +1,247 @@
+import functools
 import math
 
 import jax
 import jax.numpy as jnp
 from jax import lax
+from jax.experimental import pallas as pl
+from jax.experimental.pallas import tpu as pltpu
 from jax.sharding import PartitionSpec as P
 
 QUERY_HEADS = 48
 KEY_VALUE_HEADS = 8
 HEAD_SIZE = 128
 PAGE = 16
+MESH = pl.DeviceIdType.MESH
+CHUNKS = 4
+CHUNK = 256
+ROW_TILE = 256
+
+
+def project_kernel(nz, tok, w, out, wbuf, csend, crecv, own, xs, rown, zs, zr, ys, yr, cs, cr, ps, pr):
+    x = lax.axis_index("tp")
+    y = lax.axis_index("groups")
+    z = lax.axis_index("ep")
+    k = lax.axis_index("section")
+    q = 2 * y + k
+    rows = tok.shape[0]
+    depth = tok.shape[1]
+    steps = 2 * CHUNKS
+
+    barrier = pltpu.get_barrier_semaphore()
+    for dz in range(1, nz):
+        pl.semaphore_signal(barrier, inc=1, device_id={"ep": lax.rem(z + dz, nz)}, device_id_type=MESH)
+    pl.semaphore_signal(barrier, inc=1, device_id={"groups": 1 - y}, device_id_type=MESH)
+    pl.semaphore_signal(barrier, inc=1, device_id={"section": 1 - k}, device_id_type=MESH)
+    for c in range(2):
+        pl.semaphore_signal(barrier, inc=1, device_id={"tp": 1 - x, "section": c}, device_id_type=MESH)
+    pl.semaphore_wait(barrier, nz + 3)
+
+    def x_copy(j, c):
+        cols = pl.ds(pl.multiple_of(j * CHUNK, CHUNK), CHUNK)
+        return pltpu.make_async_remote_copy(
+            src_ref=w.at[2 * y + c, :, cols], dst_ref=wbuf.at[j, z, 2 * y + c],
+            send_sem=xs.at[j, c], recv_sem=rown.at[j],
+            device_id={"tp": 1 - x, "section": c}, device_id_type=MESH)
+
+    def peer_copy(j):
+        cols = pl.ds(pl.multiple_of(j * CHUNK, CHUNK), CHUNK)
+        return pltpu.make_async_remote_copy(
+            src_ref=w.at[2 * y + 1 - k, :, cols], dst_ref=wbuf.at[CHUNKS + j, z, 2 * y + 1 - k],
+            send_sem=xs.at[j, 0], recv_sem=rown.at[CHUNKS + j],
+            device_id={"section": 1 - k}, device_id_type=MESH)
+
+    def local_copy(j):
+        cols = pl.ds(pl.multiple_of(j * CHUNK, CHUNK), CHUNK)
+        return pltpu.make_async_copy(w.at[q, :, cols], wbuf.at[CHUNKS + j, z, q], rown.at[CHUNKS + j])
+
+    def own_wait(e):
+        return pltpu.make_async_remote_copy(
+            src_ref=wbuf.at[e, z, q], dst_ref=wbuf.at[e, z, q],
+            send_sem=xs.at[0, 0], recv_sem=rown.at[e],
+            device_id={"section": 1 - k}, device_id_type=MESH)
+
+    def z_copy(e, dz):
+        return pltpu.make_async_remote_copy(
+            src_ref=wbuf.at[e, z, q], dst_ref=wbuf.at[e, z, q],
+            send_sem=zs.at[e, dz - 1], recv_sem=zr.at[e, dz - 1],
+            device_id={"ep": lax.rem(z + dz, nz)}, device_id_type=MESH)
+
+    def z_wait(e, dz):
+        src = lax.rem(z + nz - dz, nz)
+        return pltpu.make_async_remote_copy(
+            src_ref=wbuf.at[e, src, q], dst_ref=wbuf.at[e, src, q],
+            send_sem=zs.at[e, dz - 1], recv_sem=zr.at[e, dz - 1],
+            device_id={"ep": src}, device_id_type=MESH)
+
+    def y_copy(e, part):
+        return pltpu.make_async_remote_copy(
+            src_ref=wbuf.at[e, :, part], dst_ref=wbuf.at[e, :, part],
+            send_sem=ys.at[e], recv_sem=yr.at[e],
+            device_id={"groups": 1 - y}, device_id_type=MESH)
+
+    def core_copy(e, side, part):
+        return pltpu.make_async_remote_copy(
+            src_ref=wbuf.at[e, :, part], dst_ref=wbuf.at[e, :, part],
+            send_sem=cs.at[e, side], recv_sem=cr.at[e, side],
+            device_id={"section": 1 - k}, device_id_type=MESH)
+
+    def part_copy(j):
+        return pltpu.make_async_remote_copy(
+            src_ref=csend.at[j], dst_ref=crecv.at[j],
+            send_sem=ps.at[j], recv_sem=pr.at[j],
+            device_id={"tp": 1 - x}, device_id_type=MESH)
+
+    @pl.when(k != x)
+    def _():
+        for j in range(CHUNKS):
+            x_copy(j, 0).start()
+            x_copy(j, 1).start()
+
+    @pl.when(k == x)
+    def _():
+        for j in range(CHUNKS):
+            peer_copy(j).start()
+            local_copy(j).start()
+
+    def multiply(e, tile):
+        at = pl.ds(pl.multiple_of(tile * ROW_TILE, ROW_TILE), ROW_TILE)
+        product = jnp.dot(tok[at, :], wbuf[e].reshape(depth, CHUNK), preferred_element_type=jnp.float32)
+        return at, product
+
+    def step(i, carry):
+        @pl.when(i < steps)
+        def _():
+            e = i
+
+            @pl.when((e < CHUNKS) | (k != x))
+            def _():
+                own_wait(e).wait_recv()
+
+            @pl.when((e >= CHUNKS) & (k == x))
+            def _():
+                local_copy(e - CHUNKS).wait()
+
+            for dz in range(1, nz):
+                z_copy(e, dz).start()
+
+        @pl.when((i >= 2) & (i < steps + 2))
+        def _():
+            e = i - 2
+            for dz in range(1, nz):
+                z_wait(e, dz).wait_recv()
+            y_copy(e, q).start()
+            core_copy(e, 0, q).start()
+
+        @pl.when((i >= 4) & (i < steps + 4))
+        def _():
+            e = i - 4
+            other = 2 * (1 - y) + k
+            y_copy(e, other).wait_recv()
+            core_copy(e, 1, other).start()
+
+        @pl.when(i >= 5)
+        def _():
+            e = i - 5
+            core_copy(e, 0, 2 * y + 1 - k).wait_recv()
+            core_copy(e, 1, 2 * (1 - y) + 1 - k).wait_recv()
+
+            @pl.when(e < CHUNKS)
+            def _():
+                def body(tile, c):
+                    at, product = multiply(e, tile)
+                    csend[e, at, :] = product.astype(jnp.bfloat16)
+                    return c
+                lax.fori_loop(0, rows // ROW_TILE, body, 0)
+                part_copy(e).start()
+
+            @pl.when(e >= CHUNKS)
+            def _():
+                def body(tile, c):
+                    at, product = multiply(e, tile)
+                    own[e - CHUNKS, at, :] = product
+                    return c
+                lax.fori_loop(0, rows // ROW_TILE, body, 0)
+
+        return carry
+
+    lax.fori_loop(0, steps + 5, step, 0)
+    for j in range(CHUNKS):
+        part_copy(j).wait_recv()
+        out[:, j * CHUNK:(j + 1) * CHUNK] = (own[j] + crecv[j].astype(jnp.float32)).astype(jnp.bfloat16)
+
+    @pl.when(k != x)
+    def _():
+        for j in range(CHUNKS):
+            x_copy(j, 0).wait_send()
+            x_copy(j, 1).wait_send()
+
+    @pl.when(k == x)
+    def _():
+        for j in range(CHUNKS):
+            peer_copy(j).wait_send()
+
+    def drain(e, carry):
+        for dz in range(1, nz):
+            z_copy(e, dz).wait_send()
+        y_copy(e, q).wait_send()
+        core_copy(e, 0, q).wait_send()
+        core_copy(e, 1, 2 * (1 - y) + k).wait_send()
+        return carry
+
+    lax.fori_loop(0, steps, drain, 0)
+    for j in range(CHUNKS):
+        part_copy(j).wait_send()
+
+
+def project(tokens, w_kv):
+    nz = lax.axis_size("ep")
+    rows, depth = tokens.shape
+    w_rows, width = w_kv.shape
+    quarter = w_rows // 4
+    steps = 2 * CHUNKS
+    dma = pltpu.SemaphoreType.DMA
+    vmem = pl.BlockSpec(memory_space=pltpu.VMEM)
+    return pl.pallas_call(
+        functools.partial(project_kernel, nz),
+        out_shape=jax.ShapeDtypeStruct((rows, width), jnp.bfloat16),
+        in_specs=[vmem, vmem],
+        out_specs=vmem,
+        scratch_shapes=[
+            pltpu.VMEM((steps, nz, 4, quarter, CHUNK), jnp.bfloat16),
+            pltpu.VMEM((CHUNKS, rows, CHUNK), jnp.bfloat16),
+            pltpu.VMEM((CHUNKS, rows, CHUNK), jnp.bfloat16),
+            pltpu.VMEM((CHUNKS, rows, CHUNK), jnp.float32),
+            dma((CHUNKS, 2)),
+            dma((steps,)),
+            dma((steps, nz - 1)),
+            dma((steps, nz - 1)),
+            dma((steps,)),
+            dma((steps,)),
+            dma((steps, 2)),
+            dma((steps, 2)),
+            dma((CHUNKS,)),
+            dma((CHUNKS,)),
+        ],
+        compiler_params=pltpu.CompilerParams(
+            collective_id=0, has_side_effects=True, vmem_limit_bytes=56 << 20),
+        cost_estimate=pl.CostEstimate(
+            flops=4 * rows * depth * width, bytes_accessed=16 << 20, transcendentals=0),
+        name="project",
+    )(tokens, w_kv.reshape(4, quarter, width))
 
 
 def local(tokens, w_kv, page_target, queries, decoded_keys, decoded_values):
-    gathered = lax.all_gather(tokens, "tp", axis=1, tiled=True)
     kv_width = w_kv.shape[1]
-    projected_rows = jnp.dot(
-        gathered,
-        lax.all_gather(w_kv, ("section", "ep"), axis=0, tiled=True),
-        preferred_element_type=jnp.float32,
-    )
-    page_rows = gathered.shape[0] // PAGE
+    if (lax.axis_size("groups"), lax.axis_size("section"), lax.axis_size("tp")) == (2, 2, 2):
+        projected_rows = project(tokens, w_kv)
+    else:
+        projected_rows = jnp.dot(
+            lax.all_gather(tokens, "tp", axis=1, tiled=True),
+            lax.all_gather(w_kv, ("section", "ep"), axis=0, tiled=True),
+            preferred_element_type=jnp.float32,
+        )
+    page_rows = tokens.shape[0] // PAGE
     page_data = projected_rows.astype(jnp.bfloat16).reshape(page_rows, PAGE * kv_width)
     targets = page_target[:, 0]
     dest_count = lax.axis_size(("section", "ep"))

time: 449 us -> 257 us (0.57)
  waiting for transfers between devices: 360 us -> 91.5 us
  Pallas kernels: 0 us -> 106 us
  matrix products: 31.5 us -> 12.8 us
  between operations: 13.5 us -> 0.11 us
    all_gather x2 -> x0, waiting for transfers between devices: 267 us -> none  [the longest x1 149 us: local(): gathered = lax.all_gather(tokens, 'tp', axis=1, tiled=True)]
    pallas_call x0 -> x1, Pallas kernels: none -> 106 us  [project(): pl.pallas_call(functools.partial(project_kernel, nz), out_shape=jax.Shape...]
    dot_general x1 -> x0, matrix products: 18.8 us -> none  [local(): jnp.dot(gathered, lax.all_gather(w_kv, ('section', 'ep'), axis=0, tiled=T...]
  transfers between devices with their start and end apart: 4 -> 2, of which waited for: 3 -> 1; matrix products, arithmetic and copies ran while one was open for 7% -> 4% of each run, Pallas kernels for 0% -> 41%
where the time goes in v1:
time: 257 us; the launch traced here: 256 us
  Pallas kernels  106 us (41%)
  waiting for transfers between devices  91.5 us (36%)
  local copies, waits for them, and re-layouts  27.6 us (11%)
  matrix products  12.8 us (5%)
  starting transfers between devices  12.5 us (5%)
  other arithmetic  6.12 us (2%)
    pallas_call x1, Pallas kernels, project(): pl.pallas_call(functools.partial(project_kernel, nz), out_shape=jax.Shape...  106 us
    all_to_all x1, waiting for transfers between devices, local(): lax.all_to_all(outgoing.reshape(dest_count, capacity, PAGE, kv_width), ('...  91.5 us
    slice x1, local copies, waits for them, and re-layouts, local(): prompt_values = arrived[:, :, 1]  9.63 us
    reshape x1, local copies, waits for them, and re-layouts, local(): arrived = arrived.reshape(-1, head_pairs, 2, HEAD_SIZE)  7.72 us
    all_to_all x1, starting transfers between devices, local(): lax.all_to_all(filled.reshape(dest_count, capacity), ('section', 'ep'), s...  6.33 us
    all_to_all x1, starting transfers between devices, local(): lax.all_to_all(outgoing.reshape(dest_count, capacity, PAGE, kv_width), ('...  6.18 us
    dot_general x1, matrix products, local(): jnp.einsum('gfsjt,tgd->fsgjd', prompt_weights, prompt_values, preferred_e...  5.94 us
  transfers between devices with their start and end apart: 2, of which 1 were waited for; matrix products, arithmetic and copies ran while one was open for 4% of the time, Pallas kernels for 41%

profile of v1, /device:TPU:0, one launch (start us, length us, event | category | flops | bytes accessed | tf_op | source)
XLA Modules:
  0.0 256.2 jit_solution(13667706983410975652)
XLA Ops:
  0.0 0.9 convert_reduce_fusion.1
  0.9 0.7 multiply_add_fusion
  1.7 0.7 all_to_all.10
  2.4 6.3 %all-to-all-start.1 = ((s32[8,1,16]{2,1,0:T(1,128)}), s32[8,1,16]{2,1,0:T(1,128)S(1)}, u32[]{:S(2)}, u32[]{:S(2)}) async-start(s32[8,1,16]{2,1,0:T(1,128)} %bitcast.5), calls=%async_computation.1 | async-start | bytes 8192 | tf_op jit(solution)/shard_map/all_to_all | solution.py:266
  8.7 105.5 %project.1 = bf16[1024,1024]{1,0:T(8,128)(2,1)} custom-call(bf16[1024,3072]{1,0:T(8,128)(2,1)} %tok.1, bf16[4,192,1024]{2,1,0:T(8,128)(2,1)} %bitcast.69), custom_call_target="tpu_custom_call" | custom-call | flops 12884901888 | bytes 16777216 | tf_op jit(solution)/shard_map/project/pallas_call | solution.py:205
  114.2 2.9 %reshape.67 = bf16[64,16384]{1,0:T(8,128)(2,1)S(1)} reshape(bf16[1024,1024]{1,0:T(8,128)(2,1)} %project.1) | data formatting | bytes 4194304 | tf_op jit(solution)/shard_map/reshape | solution.py:245
  117.1 1.4 convolution_convert_fusion
  118.5 4.7 %copy.98 = bf16[16,8,16,1024]{3,2,1,0:T(8,128)(2,1)} copy(bf16[16,8,16,1024]{3,1,2,0:T(8,128)(2,1)S(1)} %bitcast.67) | data formatting | bytes 8388608
  123.2 6.2 %all-to-all-start = ((bf16[8,16,16,1024]{3,2,1,0:T(8,128)(2,1)}), bf16[8,16,16,1024]{3,2,1,0:T(8,128)(2,1)}, u32[]{:S(2)}, u32[]{:S(2)}) async-start(bf16[8,16,16,1024]{3,2,1,0:T(8,128)(2,1)} %bitcast.66), calls=%async_computation | async-start | bytes 8388608 | tf_op jit(solution)/shard_map/all_to_all | solution.py:259
  129.4 0.3 reshape.70
  129.7 1.3 fusion.20
  131.0 0.1 copy.79
  131.5 91.5 %all-to-all-done = bf16[8,16,16,1024]{3,2,1,0:T(8,128)(2,1)} async-done(((bf16[8,16,16,1024]{3,2,1,0:T(8,128)(2,1)}), bf16[8,16,16,1024]{3,2,1,0:T(8,128)(2,1)}, u32[]{:S(2)}, u32[]{:S(2)}) %all-to-all-start) | async-done | bytes 4194336 | tf_op jit(solution)/shard_map/all_to_all | solution.py:259
  223.0 7.7 %reshape.69 = bf16[2048,4,2,128]{3,2,1,0:T(2,128)(2,1)} reshape(bf16[8,16,16,1024]{3,2,1,0:T(8,128)(2,1)} %all-to-all-done) | data formatting | bytes 8388608 | tf_op jit(solution)/shard_map/reshape | solution.py:275
  230.7 9.6 %fusion.19 = (bf16[2048,4,1,128]{3,2,1,0:T(2,128)(2,1)}, bf16[2048,4,1,128]{3,2,1,0:T(2,128)(2,1)S(1)}) fusion(bf16[2048,4,2,128]{3,2,1,0:T(2,128)(2,1)} %reshape.69), kind=kLoop, calls=%fused_computation.36 | loop fusion | bytes 8388608 | tf_op jit(solution)/shard_map/slice | solution.py:277
  240.4 3.8 %bitcast_reduce_fusion = (f32[4,16,2,6]{1,3,2,0:T(8,128)S(1)}, f32[4,2048,16,2,6]{1,2,4,3,0:T(8,128)}) fusion(pred[2048]{0:T(1024)(128)(4,1)S(1)} %gt.16, bf16[16,2,4,6,128]{4,3,2,0,1:T(8,128)(2,1)S(1)} %reshape.70, bf16[2048,4,1,128]{3,2,1,0:T(2,128)(2,1)S(1)} %get-tuple-element.6), kind=kOutput, calls=%fused_computation.2 | convolution fusion | flops 407371008 | bytes 8590336 | tf_op jit(solution)/shard_map/fsgjd,tgd->gfsjt/dot_general | solution.py:287
  244.2 0.1 copy.80
  244.3 4.1 %fusion.1 = f32[4,16,2,6]{1,3,2,0:T(8,128)S(1)} fusion(f32[4,2048,16,2,6]{1,2,4,3,0:T(8,128)} %get-tuple-element.8, f32[4,16,2,6]{1,3,2,0:T(8,128)S(1)} %max.7, pred[2048]{0:T(1024)(128)(4,1)S(1)} %gt.16), kind=kLoop, calls=%fused_computation.6 | loop fusion | flops 6290688 | bytes 6299648 | tf_op jit(solution)/shard_map/reduce_sum | solution.py:304
  248.5 0.3 fusion.10
  248.7 0.1 copy.81
  248.9 0.1 copy.82
  249.0 0.3 fusion.11
  249.4 5.9 %fusion.6 = bf16[16,2,4,6,128]{4,0,3,1,2:T(8,128)(2,1)S(1)} fusion(f32[4,2048,16,2,6]{1,2,4,3,0:T(8,128)} %get-tuple-element.8, f32[4,16,2,6]{1,3,2,0:T(8,128)S(1)} %add.19, f32[4,16,2,6]{1,3,2,0:T(8,128)S(1)} %max.7, pred[2048]{0:T(1024)(128)(4,1)S(1)} %gt.16, bf16[2048,4,1,128]{3,2,1,0:T(2,128)(2,1)} %get-tuple-element.5, ...), kind=kOutput, calls=%fused_computation.13 | convolution fusion | flops 410714112 | bytes 8986624 | tf_op jit(solution)/shard_map/gfsjt,tgd->fsgjd/dot_general | solution.py:307
  255.4 0.8 reshape.77
  (18 shorter events, 0.6 us)
Async XLA Ops:
  0.0 249.0 %copy-start = (bf16[16,2,512]{2,1,0:T(2,128)(2,1)S(1)}, bf16[16,2,512]{2,1,0:T(2,128)(2,1)}, u32[]{:S(2)}) copy-start(bf16[16,2,512]{2,1,0:T(2,128)(2,1)} %param.11) | copy-start | bytes 98308
  2.4 120.8 %all-to-all-start.1 = ((s32[8,1,16]{2,1,0:T(1,128)}), s32[8,1,16]{2,1,0:T(1,128)S(1)}, u32[]{:S(2)}, u32[]{:S(2)}) async-start(s32[8,1,16]{2,1,0:T(1,128)} %bitcast.5), calls=%async_computation.1 | async-start | bytes 8192 | tf_op jit(solution)/shard_map/all_to_all | solution.py:266
  123.2 6.2 %copy-start.1 = (bf16[16,2,3072]{2,1,0:T(2,128)(2,1)S(1)}, bf16[16,2,3072]{2,1,0:T(2,128)(2,1)}, u32[]{:S(2)}) copy-start(bf16[16,2,3072]{2,1,0:T(2,128)(2,1)} %param.9) | copy-start | bytes 589828
  123.2 6.5 %copy-start.2 = (bf16[16,2,512]{2,1,0:T(2,128)(2,1)S(1)}, bf16[16,2,512]{2,1,0:T(2,128)(2,1)}, u32[]{:S(2)}) copy-start(bf16[16,2,512]{2,1,0:T(2,128)(2,1)} %param.10) | copy-start | bytes 98308
  123.2 99.8 %all-to-all-start = ((bf16[8,16,16,1024]{3,2,1,0:T(8,128)(2,1)}), bf16[8,16,16,1024]{3,2,1,0:T(8,128)(2,1)}, u32[]{:S(2)}, u32[]{:S(2)}) async-start(bf16[8,16,16,1024]{3,2,1,0:T(8,128)(2,1)} %bitcast.66), calls=%async_computation | async-start | bytes 8388608 | tf_op jit(solution)/shard_map/all_to_all | solution.py:259

commit v2 on v1

--- a/solution.py
+++ b/solution.py
@@ -12,13 +12,20 @@
 KEY_VALUE_HEADS = 8
 HEAD_SIZE = 128
 PAGE = 16
+STEPS = 2
+GROUPED = QUERY_HEADS // KEY_VALUE_HEADS
 MESH = pl.DeviceIdType.MESH
 CHUNKS = 4
-CHUNK = 256
+HALF = CHUNKS // 2
+CHUNK = 2 * HEAD_SIZE
 ROW_TILE = 256
-
-
-def project_kernel(nz, tok, w, out, wbuf, csend, crecv, own, xs, rown, zs, zr, ys, yr, cs, cr, ps, pr):
+LOG2E = math.log2(math.e)
+NEVER = -1e30
+
+
+def serve_kernel(nz, tok, w, requests, qown, fresh_k, fresh_v, out, wbuf, csend, crecv, own, qall, po, pst, cpo, cpst,
+                 zo, zst, ro, rst, fo, fst, xs, rown, zs, zr, ys, yr, cs, cr, ps, pr,
+                 qs, qr, qcs, qcr, hs, hr, gs, gr, fs, fr):
     x = lax.axis_index("tp")
     y = lax.axis_index("groups")
     z = lax.axis_index("ep")
@@ -92,6 +99,135 @@
             send_sem=ps.at[j], recv_sem=pr.at[j],
             device_id={"tp": 1 - x}, device_id_type=MESH)
 
+    lanes = 2 * qown.shape[1]
+    scale = LOG2E / math.sqrt(HEAD_SIZE)
+
+    def q_copy(dz):
+        return pltpu.make_async_remote_copy(
+            src_ref=qown, dst_ref=qall.at[z, k], send_sem=qs.at[dz - 1], recv_sem=qr.at[dz - 1],
+            device_id={"ep": lax.rem(z + dz, nz)}, device_id_type=MESH)
+
+    def q_wait(dz):
+        src = lax.rem(z + nz - dz, nz)
+        return pltpu.make_async_remote_copy(
+            src_ref=qown, dst_ref=qall.at[src, k], send_sem=qs.at[dz - 1], recv_sem=qr.at[dz - 1],
+            device_id={"ep": src}, device_id_type=MESH)
+
+    def q_core(core):
+        return pltpu.make_async_remote_copy(
+            src_ref=qall.at[:, core], dst_ref=qall.at[:, core], send_sem=qcs, recv_sem=qcr,
+            device_id={"section": 1 - k}, device_id_type=MESH)
+
+    def head_copies(j):
+        return [pltpu.make_async_remote_copy(
+            src_ref=a.at[j], dst_ref=b.at[j // 2], send_sem=hs.at[j // 2, n], recv_sem=hr.at[j // 2, n],
+            device_id={"section": 1 - k}, device_id_type=MESH)
+            for n, (a, b) in enumerate([(po, cpo), (pst, cpst)])]
+
+    def chip_copies(jj, dz):
+        to = lax.rem(z + dz, nz)
+        return [pltpu.make_async_remote_copy(
+            src_ref=a.at[jj, to], dst_ref=b.at[jj, z], send_sem=gs.at[jj, dz - 1, n], recv_sem=gr.at[jj, dz - 1, n],
+            device_id={"ep": to}, device_id_type=MESH)
+            for n, (a, b) in enumerate([(zo, ro), (zst, rst)])]
+
+    def chip_waits(jj, dz):
+        src = lax.rem(z + nz - dz, nz)
+        return [pltpu.make_async_remote_copy(
+            src_ref=a.at[jj, src], dst_ref=b.at[jj, src], send_sem=gs.at[jj, dz - 1, n],
+            recv_sem=gr.at[jj, dz - 1, n], device_id={"ep": src}, device_id_type=MESH)
+            for n, (a, b) in enumerate([(zo, ro), (zst, rst)])]
+
+    def final_copies(jj, core):
+        return [pltpu.make_async_remote_copy(
+            src_ref=a.at[core, jj], dst_ref=a.at[core, jj], send_sem=fs.at[jj, n], recv_sem=fr.at[jj, n],
+            device_id={"section": 1 - k}, device_id_type=MESH)
+            for n, a in enumerate([fo, fst])]
+
+    def attend(j, keys, values):
+        lane = lax.broadcasted_iota(jnp.int32, (1, lanes), 1)
+        lane_core = (lane >= lanes // 2).astype(jnp.int32)
+        values_t = values.T
+
+        def body(block, carry):
+            heads = qall[block, :, j].reshape(lanes, HEAD_SIZE)
+            scores = lax.dot_general(keys, heads, (((1,), (1,)), ((), ())), preferred_element_type=jnp.float32)
+            mine = requests[...] == lane_core * nz + block
+            scores = jnp.where(mine, scores * scale, NEVER)
+            peak = jnp.max(scores, axis=0, keepdims=True)
+            weights = jnp.exp2(scores - peak)
+            total = jnp.sum(weights, axis=0, keepdims=True)
+            sums = jnp.dot(values_t, weights.astype(jnp.bfloat16), preferred_element_type=jnp.float32)
+            po[j, block] = sums.astype(jnp.bfloat16)
+            pst[j, block, 0:1] = peak
+            pst[j, block, 1:2] = total
+            return carry
+
+        lax.fori_loop(0, nz, body, 0)
+
+    def merge(items):
+        peak = items[0][1]
+        for item in items[1:]:
+            peak = jnp.maximum(peak, item[1])
+        factors = [jnp.exp2(item[1] - peak) for item in items]
+        total = sum(f * item[2] for f, item in zip(factors, items))
+        sums = sum(f * item[0].astype(jnp.float32) for f, item in zip(factors, items))
+        return sums, peak, total
+
+    def combine_cores(j):
+        jj = j // 2
+
+        @pl.when(k == j % 2)
+        def _():
+            for c in head_copies(j):
+                c.wait_recv()
+            for b in range(nz):
+                sums, peak, total = merge([
+                    (po[j, b], pst[j, b, 0:1], pst[j, b, 1:2]),
+                    (cpo[jj, b], cpst[jj, b, 0:1], cpst[jj, b, 1:2])])
+                zo[jj, b] = sums.astype(jnp.bfloat16)
+                zst[jj, b, 0:1] = peak
+                zst[jj, b, 1:2] = total
+            for dz in range(1, nz):
+                for c in chip_copies(jj, dz):
+                    c.start()
+
+    def combine_chips(jj):
+        items = [(zo[jj, z], zst[jj, z, 0:1], zst[jj, z, 1:2])]
+        for dz in range(1, nz):
+            for c in chip_waits(jj, dz):
+                c.wait_recv()
+            src = lax.rem(z + nz - dz, nz)
+            items.append((ro[jj, src], rst[jj, src, 0:1], rst[jj, src, 1:2]))
+        sums, peak, total = merge(items)
+        fo[k, jj] = sums.T
+        fst[k, jj, 0] = jnp.broadcast_to(peak, (HEAD_SIZE, lanes)).T
+        fst[k, jj, 1] = jnp.broadcast_to(total, (HEAD_SIZE, lanes)).T
+
+    def finish(j):
+        rows_of = pl.ds(pl.multiple_of(k * (lanes // 2), 64), lanes // 2)
+        sums = fo[j % 2, j // 2, rows_of]
+        peak = fst[j % 2, j // 2, 0, rows_of]
+        total = fst[j % 2, j // 2, 1, rows_of]
+        query = qown[j].astype(jnp.float32)
+        row = lax.broadcasted_iota(jnp.int32, (lanes // 2, 1), 0)
+        row_step = lax.rem(row // GROUPED, STEPS)
+        fresh = []
+        for u in range(STEPS):
+            s = jnp.sum(query * fresh_k[u, j].astype(jnp.float32), axis=1, keepdims=True) * scale
+            fresh.append(jnp.where(row_step >= u, s, NEVER))
+        top = peak
+        for s in fresh:
+            top = jnp.maximum(top, s)
+        fade = jnp.exp2(peak - top)
+        exps = [jnp.exp2(s - top) for s in fresh]
+        inverse = 1.0 / (fade * total + sum(exps))
+        result = sums * (fade * inverse)
+        for u in range(STEPS):
+            weight = (exps[u] * inverse).astype(jnp.bfloat16).astype(jnp.float32)
+            result = result + weight * fresh_v[u, j].astype(jnp.float32)
+        out[j] = result.astype(jnp.bfloat16)
+
     @pl.when(k != x)
     def _():
         for j in range(CHUNKS):
@@ -109,6 +245,8 @@
         product = jnp.dot(tok[at, :], wbuf[e].reshape(depth, CHUNK), preferred_element_type=jnp.float32)
         return at, product
 
+    qall[z, k] = qown[...]
+
     def step(i, carry):
         @pl.when(i < steps)
         def _():
@@ -132,6 +270,11 @@
                 z_wait(e, dz).wait_recv()
             y_copy(e, q).start()
             core_copy(e, 0, q).start()
+
+        @pl.when(i == steps)
+        def _():
+            for dz in range(1, nz):
+                q_copy(dz).start()
 
         @pl.when((i >= 4) & (i < steps + 4))
         def _():
@@ -166,9 +309,38 @@
         return carry
 
     lax.fori_loop(0, steps + 5, step, 0)
+    for dz in range(1, nz):
+        q_wait(dz).wait_recv()
+    q_core(k).start()
+    q_core(1 - k).wait_recv()
     for j in range(CHUNKS):
         part_copy(j).wait_recv()
-        out[:, j * CHUNK:(j + 1) * CHUNK] = (own[j] + crecv[j].astype(jnp.float32)).astype(jnp.bfloat16)
+        block = (own[j] + crecv[j].astype(jnp.float32)).astype(jnp.bfloat16)
+        keys, values = block[:, :HEAD_SIZE], block[:, HEAD_SIZE:]
+        attend(j, keys, values)
+
+        @pl.when(k != j % 2)
+        def _():
+            for c in head_copies(j):
+                c.start()
+
+        if j >= 1:
+            combine_cores(j - 1)
+    combine_cores(CHUNKS - 1)
+    for jj in range(HALF):
+        combine_chips(jj)
+    for jj in range(HALF):
+        for c in final_copies(jj, k):
+            c.start()
+    for j in range(CHUNKS):
+        jj = j // 2
+
+        @pl.when(k != j % 2)
+        def _():
+            for c in final_copies(jj, 1 - k):
+                c.wait_recv()
+
+        finish(j)
 
     @pl.when(k != x)
     def _():
@@ -193,55 +365,96 @@
     for j in range(CHUNKS):
         part_copy(j).wait_send()
 
-
-def project(tokens, w_kv):
+    for dz in range(1, nz):
+        q_copy(dz).wait_send()
+    q_core(k).wait_send()
+    for j in range(CHUNKS):
+        @pl.when(k != j % 2)
+        def _():
+            for c in head_copies(j):
+                c.wait_send()
+    for jj in range(HALF):
+        for dz in range(1, nz):
+            for c in chip_copies(jj, dz):
+                c.wait_send()
+        for c in final_copies(jj, k):
+            c.wait_send()
+
+
+def serve(tokens, w_kv, page_target, queries, decoded_keys, decoded_values):
     nz = lax.axis_size("ep")
     rows, depth = tokens.shape
     w_rows, width = w_kv.shape
+    forks = queries.shape[0]
     quarter = w_rows // 4
     steps = 2 * CHUNKS
+    q_rows = forks * STEPS * GROUPED
+    lanes = 2 * q_rows
+    qown = queries.reshape(forks, STEPS, CHUNKS, GROUPED, HEAD_SIZE)
+    qown = qown.transpose(2, 0, 1, 3, 4).reshape(CHUNKS, q_rows, HEAD_SIZE)
+
+    def spread(a):
+        a = a.reshape(forks, STEPS, CHUNKS, 1, HEAD_SIZE).transpose(1, 2, 0, 3, 4)
+        a = jnp.broadcast_to(a, (STEPS, CHUNKS, forks, STEPS * GROUPED, HEAD_SIZE))
+        return a.reshape(STEPS, CHUNKS, q_rows, HEAD_SIZE)
+
+    requests = jnp.repeat(page_target[:, 0], PAGE)[:, None]
     dma = pltpu.SemaphoreType.DMA
     vmem = pl.BlockSpec(memory_space=pltpu.VMEM)
-    return pl.pallas_call(
-        functools.partial(project_kernel, nz),
-        out_shape=jax.ShapeDtypeStruct((rows, width), jnp.bfloat16),
-        in_specs=[vmem, vmem],
+    bf16, f32 = jnp.bfloat16, jnp.float32
+    out = pl.pallas_call(
+        functools.partial(serve_kernel, nz),
+        out_shape=jax.ShapeDtypeStruct((CHUNKS, q_rows, HEAD_SIZE), bf16),
+        in_specs=[vmem] * 6,
         out_specs=vmem,
         scratch_shapes=[
-            pltpu.VMEM((steps, nz, 4, quarter, CHUNK), jnp.bfloat16),
-            pltpu.VMEM((CHUNKS, rows, CHUNK), jnp.bfloat16),
-            pltpu.VMEM((CHUNKS, rows, CHUNK), jnp.bfloat16),
-            pltpu.VMEM((CHUNKS, rows, CHUNK), jnp.float32),
-            dma((CHUNKS, 2)),
-            dma((steps,)),
-            dma((steps, nz - 1)),
-            dma((steps, nz - 1)),
-            dma((steps,)),
-            dma((steps,)),
-            dma((steps, 2)),
-            dma((steps, 2)),
-            dma((CHUNKS,)),
-            dma((CHUNKS,)),
+            pltpu.VMEM((steps, nz, 4, quarter, CHUNK), bf16),
+            pltpu.VMEM((CHUNKS, rows, CHUNK), bf16),
+            pltpu.VMEM((CHUNKS, rows, CHUNK), bf16),
+            pltpu.VMEM((CHUNKS, rows, CHUNK), f32),
+            pltpu.VMEM((nz, 2, CHUNKS, q_rows, HEAD_SIZE), bf16),
+            pltpu.VMEM((CHUNKS, nz, HEAD_SIZE, lanes), bf16),
+            pltpu.VMEM((CHUNKS, nz, 8, lanes), f32),
+            pltpu.VMEM((HALF, nz, HEAD_SIZE, lanes), bf16),
+            pltpu.VMEM((HALF, nz, 8, lanes), f32),
+            pltpu.VMEM((HALF, nz, HEAD_SIZE, lanes), bf16),
+            pltpu.VMEM((HALF, nz, 8, lanes), f32),
+            pltpu.VMEM((HALF, nz, HEAD_SIZE, lanes), bf16),
+            pltpu.VMEM((HALF, nz, 8, lanes), f32),
+            pltpu.VMEM((2, HALF, lanes, HEAD_SIZE), f32),
+            pltpu.VMEM((2, HALF, 2, lanes, HEAD_SIZE), f32),
+            dma((CHUNKS, 2)), dma((steps,)),
+            dma((steps, nz - 1)), dma((steps, nz - 1)),
+            dma((steps,)), dma((steps,)),
+            dma((steps, 2)), dma((steps, 2)),
+            dma((CHUNKS,)), dma((CHUNKS,)),
+            dma((nz - 1,)), dma((nz - 1,)), dma, dma,
+            dma((HALF, 2)), dma((HALF, 2)),
+            dma((HALF, nz - 1, 2)), dma((HALF, nz - 1, 2)),
+            dma((HALF, 2)), dma((HALF, 2)),
         ],
         compiler_params=pltpu.CompilerParams(
-            collective_id=0, has_side_effects=True, vmem_limit_bytes=56 << 20),
+            collective_id=0, has_side_effects=True, vmem_limit_bytes=60 << 20),
         cost_estimate=pl.CostEstimate(
             flops=4 * rows * depth * width, bytes_accessed=16 << 20, transcendentals=0),
-        name="project",
-    )(tokens, w_kv.reshape(4, quarter, width))
+        name="serve",
+    )(tokens, w_kv.reshape(4, quarter, width), requests, qown, spread(decoded_keys), spread(decoded_values))
+    out = out.reshape(CHUNKS, forks, STEPS, GROUPED, HEAD_SIZE).transpose(1, 2, 0, 3, 4)
+    return out.reshape(forks, STEPS, CHUNKS * GROUPED * HEAD_SIZE)
 
 
 def local(tokens, w_kv, page_target, queries, decoded_keys, decoded_values):
+    axes = tuple(lax.axis_size(a) for a in ("groups", "section", "tp"))
+    if axes == (2, 2, 2) and w_kv.shape[1] == CHUNKS * CHUNK:
+        return serve(tokens, w_kv, page_target, queries, decoded_keys, decoded_values)
+    gathered = lax.all_gather(tokens, "tp", axis=1, tiled=True)
     kv_width = w_kv.shape[1]
-    if (lax.axis_size("groups"), lax.axis_size("section"), lax.axis_size("tp")) == (2, 2, 2):
-        projected_rows = project(tokens, w_kv)
-    else:
-        projected_rows = jnp.dot(
-            lax.all_gather(tokens, "tp", axis=1, tiled=True),
-            lax.all_gather(w_kv, ("section", "ep"), axis=0, tiled=True),
-            preferred_element_type=jnp.float32,
-        )
-    page_rows = tokens.shape[0] // PAGE
+    projected_rows = jnp.dot(
+        gathered,
+        lax.all_gather(w_kv, ("section", "ep"), axis=0, tiled=True),
+        preferred_element_type=jnp.float32,
+    )
+    page_rows = gathered.shape[0] // PAGE
     page_data = projected_rows.astype(jnp.bfloat16).reshape(page_rows, PAGE * kv_width)
     targets = page_target[:, 0]
     dest_count = lax.axis_size(("section", "ep"))

time: 257 us -> 150 us (0.58)
  waiting for transfers between devices: 91.5 us -> 0 us
  Pallas kernels: 106 us -> 140 us
  local copies, waits for them, and re-layouts: 27.6 us -> 9.18 us
  matrix products: 12.8 us -> 0 us
  starting transfers between devices: 12.5 us -> 0 us
  other arithmetic: 6.12 us -> 0 us
    all_to_all x2 -> x0, waiting for transfers between devices: 91.5 us -> none  [the longest x1 91.5 us: local(): lax.all_to_all(outgoing.reshape(dest_count, capacity, PAGE, kv_width), ('...]
    pallas_call x1, Pallas kernels: 106 us -> 140 us  [serve(): pl.pallas_call(functools.partial(serve_kernel, nz), out_shape=jax.ShapeDt...]
    dot_general x5 -> x0, matrix products: 12.8 us -> none  [the longest x1 5.94 us: local(): jnp.einsum('gfsjt,tgd->fsgjd', prompt_weights, prompt_values, preferred_e...]
    all_to_all x2 -> x0, starting transfers between devices: 12.5 us -> none  [the longest x1 6.33 us: local(): lax.all_to_all(filled.reshape(dest_count, capacity), ('section', 'ep'), s...]
    slice x1 -> x0, local copies, waits for them, and re-layouts: 9.63 us -> none  [local(): prompt_values = arrived[:, :, 1]]
    reshape x4 -> x8, local copies, waits for them, and re-layouts: 10.9 us -> 5.01 us  [the longest x2 1.62 us: spread(): return a.reshape(STEPS, CHUNKS, q_rows, HEAD_SIZE)]
    reduce_sum x4 -> x0, other arithmetic: 5.41 us -> none  [the longest x1 4.15 us: local(): jnp.sum(prompt_exp, -1, keepdims=True)]
    unnamed x8 -> x1, local copies, waits for them, and re-layouts: 4.76 us -> 0.96 us
  transfers between devices with their start and end apart: 2 -> 0, of which waited for: 1 -> 0; matrix products, arithmetic and copies ran while one was open for 4% -> 0% of each run, Pallas kernels for 41% -> 0%
where the time goes in v2:
time: 150 us
  Pallas kernels  140 us (93%)
  local copies, waits for them, and re-layouts  9.18 us (6%)
    pallas_call x1, Pallas kernels, serve(): pl.pallas_call(functools.partial(serve_kernel, nz), out_shape=jax.ShapeDt...  140 us

profile of v2, /device:TPU:0, one launch (start us, length us, event | category | flops | bytes accessed | tf_op | source)
XLA Modules:
  0.0 149.6 jit_solution(9027684951016510286)
XLA Ops:
  0.0 0.7 broadcast_in_dim.17
  0.7 0.8 reshape.30
  1.5 0.8 reshape.32
  2.3 1.0 copy.11
  3.3 0.3 reshape.28
  3.6 0.1 copy.12
  3.7 0.7 copy.16.qown
  4.4 0.1 broadcast_in_dim.21
  4.5 0.8 copy.18.fresh_v
  5.3 0.1 broadcast_in_dim.19
  5.4 0.8 copy.17.fresh_k
  6.2 1.1 broadcast_in_dim_reshape.4.requests
  7.3 140.4 %serve.1 = bf16[4,192,128]{2,1,0:T(8,128)(2,1)} custom-call(bf16[1024,3072]{1,0:T(8,128)(2,1)} %tok.1, bf16[4,192,1024]{2,1,0:T(8,128)(2,1)} %bitcast.25, s32[1024,1]{1,0:T(8,128)} %broadcast_in_dim_reshape.4.requests, bf16[4,192,128]{2,1,0:T(8,128)(2,1)} %copy.16.qown, bf16[2,4,192,128]{3,2,1,0:T(8,128)(2,1)} %copy.17.fresh_k, ...), custom_call_target="tpu_custom_call" | custom-call | flops 12884901888 | bytes 16777216 | tf_op jit(solution)/shard_map/serve/pallas_call | solution.py:405
  147.7 1.1 copy.19
  148.8 0.1 copy.22
  148.8 0.8 reshape.36
  (2 shorter events, 0.0 us)

commit v3 on v2

--- a/solution.py
+++ b/solution.py
@@ -21,16 +21,20 @@
 ROW_TILE = 256
 LOG2E = math.log2(math.e)
 NEVER = -1e30
-
-
-def serve_kernel(nz, tok, w, requests, qown, fresh_k, fresh_v, out, wbuf, csend, crecv, own, qall, po, pst, cpo, cpst,
+AHEAD = 2
+SKEW_Y = 3
+SKEW_M = 3
+
+
+def serve_kernel(nz, tok_hbm, w, requests, qown, fresh_k, fresh_v, out, tok, wbuf, csend, crecv, kv, qall, po, pst, cpo, cpst,
                  zo, zst, ro, rst, fo, fst, xs, rown, zs, zr, ys, yr, cs, cr, ps, pr,
-                 qs, qr, qcs, qcr, hs, hr, gs, gr, fs, fr):
+                 qs, qr, qcs, qcr, hs, hr, gs, gr, fs, fr, ts):
     x = lax.axis_index("tp")
     y = lax.axis_index("groups")
     z = lax.axis_index("ep")
     k = lax.axis_index("section")
     q = 2 * y + k
+    forks = fresh_k.shape[1]
     rows = tok.shape[0]
     depth = tok.shape[1]
     steps = 2 * CHUNKS
@@ -42,6 +46,8 @@
     pl.semaphore_signal(barrier, inc=1, device_id={"section": 1 - k}, device_id_type=MESH)
     for c in range(2):
         pl.semaphore_signal(barrier, inc=1, device_id={"tp": 1 - x, "section": c}, device_id_type=MESH)
+    tok_copy = pltpu.make_async_copy(tok_hbm, tok, ts)
+    tok_copy.start()
     pl.semaphore_wait(barrier, nz + 3)
 
     def x_copy(j, c):
@@ -54,44 +60,99 @@
     def peer_copy(j):
         cols = pl.ds(pl.multiple_of(j * CHUNK, CHUNK), CHUNK)
         return pltpu.make_async_remote_copy(
-            src_ref=w.at[2 * y + 1 - k, :, cols], dst_ref=wbuf.at[CHUNKS + j, z, 2 * y + 1 - k],
+            src_ref=w.at[:, :, cols], dst_ref=wbuf.at[CHUNKS + j, z],
             send_sem=xs.at[j, 0], recv_sem=rown.at[CHUNKS + j],
             device_id={"section": 1 - k}, device_id_type=MESH)
 
     def local_copy(j):
         cols = pl.ds(pl.multiple_of(j * CHUNK, CHUNK), CHUNK)
-        return pltpu.make_async_copy(w.at[q, :, cols], wbuf.at[CHUNKS + j, z, q], rown.at[CHUNKS + j])
-
-    def own_wait(e):
+        return pltpu.make_async_copy(w.at[:, :, cols], wbuf.at[CHUNKS + j, z], rown.at[CHUNKS + j])
+
+    def z_hop(e):
+        def hop(src, right):
+            block = wbuf.at[e, src, q]
+            return pltpu.make_async_remote_copy(
+                src_ref=block, dst_ref=block, send_sem=zs.at[e, src, right], recv_sem=zr.at[e, src],
+                device_id={"ep": lax.rem(z + 1 if right else z + nz - 1, nz)}, device_id_type=MESH)
+        return hop
+
+    def q_hop(src, right):
+        block = qall.at[src, k]
         return pltpu.make_async_remote_copy(
-            src_ref=wbuf.at[e, z, q], dst_ref=wbuf.at[e, z, q],
-            send_sem=xs.at[0, 0], recv_sem=rown.at[e],
+            src_ref=block, dst_ref=block, send_sem=qs.at[src, right], recv_sem=qr.at[src],
+            device_id={"ep": lax.rem(z + 1 if right else z + nz - 1, nz)}, device_id_type=MESH)
+
+    def send_own(hop):
+        @pl.when(z < nz - 1)
+        def _():
+            hop(z, 1).start()
+
+        @pl.when(z > 0)
+        def _():
+            hop(z, 0).start()
+
+    def pass_on(hop, d, then):
+        @pl.when(z - d >= 0)
+        def _():
+            hop(z - d, 1).wait_recv()
+
+            @pl.when(z < nz - 1)
+            def _():
+                hop(z - d, 1).start()
+            then(z - d)
+
+        @pl.when(z + d < nz)
+        def _():
+            hop(z + d, 0).wait_recv()
+
+            @pl.when(z > 0)
+            def _():
+                hop(z + d, 0).start()
+            then(z + d)
+
+    def drain_hops(hop):
+        @pl.when(z < nz - 1)
+        def _():
+            hop(z, 1).wait_send()
+
+        @pl.when(z > 0)
+        def _():
+            hop(z, 0).wait_send()
+
+        for d in range(1, nz):
+            @pl.when((z - d >= 0) & (z < nz - 1))
+            def _():
+                hop(z - d, 1).wait_send()
+
+            @pl.when((z + d < nz) & (z > 0))
+            def _():
+                hop(z + d, 0).wait_send()
+
+    def y_copy(e, src, part):
+        return pltpu.make_async_remote_copy(
+            src_ref=wbuf.at[e, src, part], dst_ref=wbuf.at[e, src, part],
+            send_sem=ys.at[e, src], recv_sem=yr.at[e, src],
+            device_id={"groups": 1 - y}, device_id_type=MESH)
+
+    def core_copy(e, side, src, part):
+        return pltpu.make_async_remote_copy(
+            src_ref=wbuf.at[e, src, part], dst_ref=wbuf.at[e, src, part],
+            send_sem=cs.at[e, side, src], recv_sem=cr.at[e, side, src],
             device_id={"section": 1 - k}, device_id_type=MESH)
 
-    def z_copy(e, dz):
-        return pltpu.make_async_remote_copy(
-            src_ref=wbuf.at[e, z, q], dst_ref=wbuf.at[e, z, q],
-            send_sem=zs.at[e, dz - 1], recv_sem=zr.at[e, dz - 1],
-            device_id={"ep": lax.rem(z + dz, nz)}, device_id_type=MESH)
-
-    def z_wait(e, dz):
-        src = lax.rem(z + nz - dz, nz)
-        return pltpu.make_async_remote_copy(
-            src_ref=wbuf.at[e, src, q], dst_ref=wbuf.at[e, src, q],
-            send_sem=zs.at[e, dz - 1], recv_sem=zr.at[e, dz - 1],
-            device_id={"ep": src}, device_id_type=MESH)
-
-    def y_copy(e, part):
-        return pltpu.make_async_remote_copy(
-            src_ref=wbuf.at[e, :, part], dst_ref=wbuf.at[e, :, part],
-            send_sem=ys.at[e], recv_sem=yr.at[e],
-            device_id={"groups": 1 - y}, device_id_type=MESH)
-
-    def core_copy(e, side, part):
-        return pltpu.make_async_remote_copy(
-            src_ref=wbuf.at[e, :, part], dst_ref=wbuf.at[e, :, part],
-            send_sem=cs.at[e, side], recv_sem=cr.at[e, side],
-            device_id={"section": 1 - k}, device_id_type=MESH)
+    def share(e, src):
+        y_copy(e, src, q).start()
+        core_copy(e, 0, src, q).start()
+
+    def each_source(e, what):
+        for d in range(nz):
+            src = lax.rem(z + d, nz)
+            if d == 0:
+                @pl.when(e < CHUNKS)
+                def _():
+                    what(src)
+            else:
+                what(src)
 
     def part_copy(j):
         return pltpu.make_async_remote_copy(
@@ -102,17 +163,6 @@
     lanes = 2 * qown.shape[1]
     scale = LOG2E / math.sqrt(HEAD_SIZE)
 
-    def q_copy(dz):
-        return pltpu.make_async_remote_copy(
-            src_ref=qown, dst_ref=qall.at[z, k], send_sem=qs.at[dz - 1], recv_sem=qr.at[dz - 1],
-            device_id={"ep": lax.rem(z + dz, nz)}, device_id_type=MESH)
-
-    def q_wait(dz):
-        src = lax.rem(z + nz - dz, nz)
-        return pltpu.make_async_remote_copy(
-            src_ref=qown, dst_ref=qall.at[src, k], send_sem=qs.at[dz - 1], recv_sem=qr.at[dz - 1],
-            device_id={"ep": src}, device_id_type=MESH)
-
     def q_core(core):
         return pltpu.make_async_remote_copy(
             src_ref=qall.at[:, core], dst_ref=qall.at[:, core], send_sem=qcs, recv_sem=qcr,
@@ -120,7 +170,8 @@
 
     def head_copies(j):
         return [pltpu.make_async_remote_copy(
-            src_ref=a.at[j], dst_ref=b.at[j // 2], send_sem=hs.at[j // 2, n], recv_sem=hr.at[j // 2, n],
+            src_ref=a.at[j], dst_ref=b.at[lax.div(j, 2)], send_sem=hs.at[lax.div(j, 2), n],
+            recv_sem=hr.at[lax.div(j, 2), n],
             device_id={"section": 1 - k}, device_id_type=MESH)
             for n, (a, b) in enumerate([(po, cpo), (pst, cpst)])]
 
@@ -144,10 +195,11 @@
             device_id={"section": 1 - k}, device_id_type=MESH)
             for n, a in enumerate([fo, fst])]
 
-    def attend(j, keys, values):
+    def attend(j):
         lane = lax.broadcasted_iota(jnp.int32, (1, lanes), 1)
         lane_core = (lane >= lanes // 2).astype(jnp.int32)
-        values_t = values.T
+        keys = kv[:, :HEAD_SIZE]
+        values_t = kv[:, HEAD_SIZE:].T
 
         def body(block, carry):
             heads = qall[block, :, j].reshape(lanes, HEAD_SIZE)
@@ -175,9 +227,9 @@
         return sums, peak, total
 
     def combine_cores(j):
-        jj = j // 2
-
-        @pl.when(k == j % 2)
+        jj = lax.div(j, 2)
+
+        @pl.when(k == lax.rem(j, 2))
         def _():
             for c in head_copies(j):
                 c.wait_recv()
@@ -211,10 +263,13 @@
         total = fst[j % 2, j // 2, 1, rows_of]
         query = qown[j].astype(jnp.float32)
         row = lax.broadcasted_iota(jnp.int32, (lanes // 2, 1), 0)
-        row_step = lax.rem(row // GROUPED, STEPS)
+        row_step = lax.rem(row // forks, STEPS)
+        head = slice(j * HEAD_SIZE, (j + 1) * HEAD_SIZE)
+        copies = lanes // 2 // forks
         fresh = []
         for u in range(STEPS):
-            s = jnp.sum(query * fresh_k[u, j].astype(jnp.float32), axis=1, keepdims=True) * scale
+            latest = jnp.concatenate([fresh_k[u, :, head].astype(jnp.float32)] * copies, axis=0)
+            s = jnp.sum(query * latest, axis=1, keepdims=True) * scale
             fresh.append(jnp.where(row_step >= u, s, NEVER))
         top = peak
         for s in fresh:
@@ -225,7 +280,8 @@
         result = sums * (fade * inverse)
         for u in range(STEPS):
             weight = (exps[u] * inverse).astype(jnp.bfloat16).astype(jnp.float32)
-            result = result + weight * fresh_v[u, j].astype(jnp.float32)
+            latest = jnp.concatenate([fresh_v[u, :, head].astype(jnp.float32)] * copies, axis=0)
+            result = result + weight * latest
         out[j] = result.astype(jnp.bfloat16)
 
     @pl.when(k != x)
@@ -247,47 +303,97 @@
 
     qall[z, k] = qown[...]
 
+    def begin(e):
+        @pl.when(e < CHUNKS)
+        def _():
+            block = wbuf.at[e, z, q]
+            pltpu.make_async_remote_copy(
+                src_ref=block, dst_ref=block, send_sem=xs.at[0, 0], recv_sem=rown.at[e],
+                device_id={"section": 1 - k}, device_id_type=MESH).wait_recv()
+            send_own(z_hop(e))
+            share(e, z)
+
+        @pl.when(e >= CHUNKS)
+        def _():
+            @pl.when(k != x)
+            def _():
+                peer_copy(e - CHUNKS).wait_recv()
+
+            @pl.when(k == x)
+            def _():
+                local_copy(e - CHUNKS).wait()
+
+            send_own(z_hop(e))
+
+    for e in range(AHEAD):
+        begin(jnp.int32(e))
+    tok_copy.wait()
+
+    def own_head(j):
+        part_copy(j).wait_recv()
+
+        def body(tile, c):
+            at, product = multiply(CHUNKS + j, tile)
+            kv[at, :] = (product + crecv[j, at, :].astype(jnp.float32)).astype(jnp.bfloat16)
+            return c
+        lax.fori_loop(0, rows // ROW_TILE, body, 0)
+
+        @pl.when(j == 0)
+        def _():
+            q_core(1 - k).wait_recv()
+
+        attend(j)
+
+        @pl.when(k != lax.rem(j, 2))
+        def _():
+            for c in head_copies(j):
+                c.start()
+
+        @pl.when(j >= 1)
+        def _():
+            combine_cores(j - 1)
+
     def step(i, carry):
-        @pl.when(i < steps)
-        def _():
-            e = i
-
-            @pl.when((e < CHUNKS) | (k != x))
-            def _():
-                own_wait(e).wait_recv()
-
-            @pl.when((e >= CHUNKS) & (k == x))
-            def _():
-                local_copy(e - CHUNKS).wait()
-
-            for dz in range(1, nz):
-                z_copy(e, dz).start()
-
-        @pl.when((i >= 2) & (i < steps + 2))
-        def _():
-            e = i - 2
-            for dz in range(1, nz):
-                z_wait(e, dz).wait_recv()
-            y_copy(e, q).start()
-            core_copy(e, 0, q).start()
-
-        @pl.when(i == steps)
-        def _():
-            for dz in range(1, nz):
-                q_copy(dz).start()
-
-        @pl.when((i >= 4) & (i < steps + 4))
-        def _():
-            e = i - 4
+        @pl.when(i + AHEAD < steps)
+        def _():
+            begin(i + AHEAD)
+
+        @pl.when(i == 1)
+        def _():
+            send_own(q_hop)
+
+        for d in range(1, nz):
+            @pl.when((i >= d - 1) & (i < steps + d - 1))
+            def _():
+                e = i - (d - 1)
+                pass_on(z_hop(e), d, functools.partial(share, e))
+
+            @pl.when(i == d + 1)
+            def _():
+                pass_on(q_hop, d, lambda src: None)
+
+        @pl.when(i == nz)
+        def _():
+            q_core(k).start()
+
+        @pl.when((i >= SKEW_Y) & (i < steps + SKEW_Y))
+        def _():
+            e = i - SKEW_Y
             other = 2 * (1 - y) + k
-            y_copy(e, other).wait_recv()
-            core_copy(e, 1, other).start()
-
-        @pl.when(i >= 5)
-        def _():
-            e = i - 5
-            core_copy(e, 0, 2 * y + 1 - k).wait_recv()
-            core_copy(e, 1, 2 * (1 - y) + 1 - k).wait_recv()
+
+            def forward(src):
+                y_copy(e, src, other).wait_recv()
+                core_copy(e, 1, src, other).start()
+            each_source(e, forward)
+
+        @pl.when(i >= SKEW_M)
+        def _():
+            e = i - SKEW_M
+
+            def arrive(src):
+                core_copy(e, 0, src, 2 * y + 1 - k).wait_recv()
+                core_copy(e, 1, src, 2 * (1 - y) + 1 - k).wait_recv()
+            each_source(e, arrive)
 
             @pl.when(e < CHUNKS)
             def _():
@@ -300,36 +406,14 @@
 
             @pl.when(e >= CHUNKS)
             def _():
-                def body(tile, c):
-                    at, product = multiply(e, tile)
-                    own[e - CHUNKS, at, :] = product
-                    return c
-                lax.fori_loop(0, rows // ROW_TILE, body, 0)
+                own_head(e - CHUNKS)
 
         return carry
 
-    lax.fori_loop(0, steps + 5, step, 0)
-    for dz in range(1, nz):
-        q_wait(dz).wait_recv()
-    q_core(k).start()
-    q_core(1 - k).wait_recv()
-    for j in range(CHUNKS):
-        part_copy(j).wait_recv()
-        block = (own[j] + crecv[j].astype(jnp.float32)).astype(jnp.bfloat16)
-        keys, values = block[:, :HEAD_SIZE], block[:, HEAD_SIZE:]
-        attend(j, keys, values)
-
-        @pl.when(k != j % 2)
-        def _():
-            for c in head_copies(j):
-                c.start()
-
-        if j >= 1:
-            combine_cores(j - 1)
-    combine_cores(CHUNKS - 1)
+    lax.fori_loop(0, steps + SKEW_M, step, 0)
+    combine_cores(jnp.int32(CHUNKS - 1))
     for jj in range(HALF):
         combine_chips(jj)
-    for jj in range(HALF):
         for c in final_copies(jj, k):
             c.start()
     for j in range(CHUNKS):
@@ -354,24 +438,25 @@
             peer_copy(j).wait_send()
 
     def drain(e, carry):
-        for dz in range(1, nz):
-            z_copy(e, dz).wait_send()
-        y_copy(e, q).wait_send()
-        core_copy(e, 0, q).wait_send()
-        core_copy(e, 1, 2 * (1 - y) + k).wait_send()
+        drain_hops(z_hop(e))
+
+        def sent(src):
+            y_copy(e, src, q).wait_send()
+            core_copy(e, 0, src, q).wait_send()
+            core_copy(e, 1, src, 2 * (1 - y) + k).wait_send()
+        each_source(e, sent)
         return carry
 
     lax.fori_loop(0, steps, drain, 0)
     for j in range(CHUNKS):
         part_copy(j).wait_send()
 
-    for dz in range(1, nz):
-        q_copy(dz).wait_send()
+    drain_hops(q_hop)
     q_core(k).wait_send()
     for j in range(CHUNKS):
         @pl.when(k != j % 2)
         def _():
-            for c in head_copies(j):
+            for c in head_copies(jnp.int32(j)):
                 c.wait_send()
     for jj in range(HALF):
         for dz in range(1, nz):
@@ -391,12 +476,7 @@
     q_rows = forks * STEPS * GROUPED
     lanes = 2 * q_rows
     qown = queries.reshape(forks, STEPS, CHUNKS, GROUPED, HEAD_SIZE)
-    qown = qown.transpose(2, 0, 1, 3, 4).reshape(CHUNKS, q_rows, HEAD_SIZE)
-
-    def spread(a):
-        a = a.reshape(forks, STEPS, CHUNKS, 1, HEAD_SIZE).transpose(1, 2, 0, 3, 4)
-        a = jnp.broadcast_to(a, (STEPS, CHUNKS, forks, STEPS * GROUPED, HEAD_SIZE))
-        return a.reshape(STEPS, CHUNKS, q_rows, HEAD_SIZE)
+    qown = qown.transpose(2, 3, 1, 0, 4).reshape(CHUNKS, q_rows, HEAD_SIZE)
 
     requests = jnp.repeat(page_target[:, 0], PAGE)[:, None]
     dma = pltpu.SemaphoreType.DMA
@@ -405,13 +485,14 @@
     out = pl.pallas_call(
         functools.partial(serve_kernel, nz),
         out_shape=jax.ShapeDtypeStruct((CHUNKS, q_rows, HEAD_SIZE), bf16),
-        in_specs=[vmem] * 6,
+        in_specs=[pl.BlockSpec(memory_space=pl.ANY)] * 2 + [vmem] * 4,
         out_specs=vmem,
         scratch_shapes=[
+            pltpu.VMEM((rows, depth), bf16),
             pltpu.VMEM((steps, nz, 4, quarter, CHUNK), bf16),
             pltpu.VMEM((CHUNKS, rows, CHUNK), bf16),
             pltpu.VMEM((CHUNKS, rows, CHUNK), bf16),
-            pltpu.VMEM((CHUNKS, rows, CHUNK), f32),
+            pltpu.VMEM((rows, CHUNK), bf16),
             pltpu.VMEM((nz, 2, CHUNKS, q_rows, HEAD_SIZE), bf16),
             pltpu.VMEM((CHUNKS, nz, HEAD_SIZE, lanes), bf16),
             pltpu.VMEM((CHUNKS, nz, 8, lanes), f32),
@@ -424,22 +505,22 @@
             pltpu.VMEM((2, HALF, lanes, HEAD_SIZE), f32),
             pltpu.VMEM((2, HALF, 2, lanes, HEAD_SIZE), f32),
             dma((CHUNKS, 2)), dma((steps,)),
-            dma((steps, nz - 1)), dma((steps, nz - 1)),
-            dma((steps,)), dma((steps,)),
-            dma((steps, 2)), dma((steps, 2)),
+            dma((steps, nz, 2)), dma((steps, nz)),
+            dma((steps, nz)), dma((steps, nz)),
+            dma((steps, 2, nz)), dma((steps, 2, nz)),
             dma((CHUNKS,)), dma((CHUNKS,)),
-            dma((nz - 1,)), dma((nz - 1,)), dma, dma,
+            dma((nz, 2)), dma((nz,)), dma, dma,
             dma((HALF, 2)), dma((HALF, 2)),
             dma((HALF, nz - 1, 2)), dma((HALF, nz - 1, 2)),
-            dma((HALF, 2)), dma((HALF, 2)),
+            dma((HALF, 2)), dma((HALF, 2)), dma,
         ],
         compiler_params=pltpu.CompilerParams(
             collective_id=0, has_side_effects=True, vmem_limit_bytes=60 << 20),
         cost_estimate=pl.CostEstimate(
             flops=4 * rows * depth * width, bytes_accessed=16 << 20, transcendentals=0),
         name="serve",
-    )(tokens, w_kv.reshape(4, quarter, width), requests, qown, spread(decoded_keys), spread(decoded_values))
-    out = out.reshape(CHUNKS, forks, STEPS, GROUPED, HEAD_SIZE).transpose(1, 2, 0, 3, 4)
+    )(tokens, w_kv.reshape(4, quarter, width), requests, qown, decoded_keys.transpose(1, 0, 2), decoded_values.transpose(1, 0, 2))
+    out = out.reshape(CHUNKS, GROUPED, STEPS, forks, HEAD_SIZE).transpose(3, 2, 0, 1, 4)
     return out.reshape(forks, STEPS, CHUNKS * GROUPED * HEAD_SIZE)
 
 

time: 150 us -> 126 us (0.84)
  Pallas kernels: 140 us -> 118 us
  local copies, waits for them, and re-layouts: 9.18 us -> 7.32 us
    pallas_call x1, Pallas kernels: 140 us -> 118 us  [serve(): pl.pallas_call(functools.partial(serve_kernel, nz), out_shape=jax.ShapeDt...]
    reshape x5 -> x1, local copies, waits for them, and re-layouts: 3.9 us -> 1.02 us  [serve(): out.reshape(CHUNKS, GROUPED, STEPS, forks, HEAD_SIZE)]
    transpose x1 -> x2, local copies, waits for them, and re-layouts: 0.08 us -> 2.16 us  [the longest x1 1.41 us: serve(): decoded_values.transpose(1, 0, 2)]
where the time goes in v3:
time: 126 us; the launch traced here: 125 us
  Pallas kernels  118 us (94%)
  local copies, waits for them, and re-layouts  7.32 us (6%)
    pallas_call x1, Pallas kernels, serve(): pl.pallas_call(functools.partial(serve_kernel, nz), out_shape=jax.ShapeDt...  118 us

profile of v3, /device:TPU:0, one launch (start us, length us, event | category | flops | bytes accessed | tf_op | source)
XLA Modules:
  0.0 125.1 jit_solution(10855314035163193629)
XLA Ops:
  0.0 0.7 broadcast_in_dim.3
  0.7 1.4 %copy_bitcast_fusion.1 = (bf16[2,16,512]{2,1,0:T(8,128)(2,1)}, bf16[2,16,512]{2,1,0:T(8,128)(2,1)}) fusion(bf16[16,2,512]{2,1,0:T(2,128)(2,1)} %param.11, bf16[16,2,512]{2,1,0:T(2,128)(2,1)} %param.10), kind=kLoop, calls=%fused_computation.1 | loop fusion | bytes 131072 | tf_op jit(solution)/shard_map/transpose | solution.py:522
  2.1 1.0 copy.11
  3.1 0.3 reshape.16
  3.4 0.8 copy.12
  4.1 1.1 broadcast_in_dim_reshape.4.requests
  5.2 117.8 %serve.1 = bf16[4,192,128]{2,1,0:T(8,128)(2,1)} custom-call(bf16[1024,3072]{1,0:T(8,128)(2,1)} %tok_hbm.1, bf16[4,192,1024]{2,1,0:T(8,128)(2,1)} %bitcast.21, s32[1024,1]{1,0:T(8,128)} %broadcast_in_dim_reshape.4.requests, bf16[4,192,128]{2,1,0:T(8,128)(2,1)} %bitcast.18, bf16[2,16,512]{2,1,0:T(8,128)(2,1)} %get-tuple-element.6.fresh_k, ...), custom_call_target="tpu_custom_call" | custom-call | flops 12884901888 | bytes 16777216 | tf_op jit(solution)/shard_map/serve/pallas_call | solution.py:485
  123.0 1.0 copy.21
  124.0 0.2 reshape.19
  124.2 0.9 copy.17

commit v4 on v3

--- a/solution.py
+++ b/solution.py
@@ -21,7 +21,7 @@
 ROW_TILE = 256
 LOG2E = math.log2(math.e)
 NEVER = -1e30
-AHEAD = 2
+AHEAD = 1
 SKEW_Y = 3
 SKEW_M = 3
 

time: 126 us -> 124 us (0.984)
  Pallas kernels: 118 us -> 116 us
    pallas_call x1, Pallas kernels: 118 us -> 116 us  [serve(): pl.pallas_call(functools.partial(serve_kernel, nz), out_shape=jax.ShapeDt...]
where the time goes in v4:
time: 124 us; the launch traced here: 123 us
  Pallas kernels  116 us (94%)
  local copies, waits for them, and re-layouts  7.32 us (6%)
    pallas_call x1, Pallas kernels, serve(): pl.pallas_call(functools.partial(serve_kernel, nz), out_shape=jax.ShapeDt...  116 us

profile of v4, /device:TPU:0, one launch (start us, length us, event | category | flops | bytes accessed | tf_op | source)
XLA Modules:
  0.0 123.4 jit_solution(1437230583999430313)
XLA Ops:
  0.0 0.7 broadcast_in_dim.3
  0.7 1.4 %copy_bitcast_fusion.1 = (bf16[2,16,512]{2,1,0:T(8,128)(2,1)}, bf16[2,16,512]{2,1,0:T(8,128)(2,1)}) fusion(bf16[16,2,512]{2,1,0:T(2,128)(2,1)} %param.11, bf16[16,2,512]{2,1,0:T(2,128)(2,1)} %param.10), kind=kLoop, calls=%fused_computation.1 | loop fusion | bytes 131072 | tf_op jit(solution)/shard_map/transpose | solution.py:522
  2.1 1.0 copy.11
  3.1 0.3 reshape.16
  3.4 0.8 copy.12
  4.1 1.1 broadcast_in_dim_reshape.4.requests
  5.2 116.1 %serve.1 = bf16[4,192,128]{2,1,0:T(8,128)(2,1)} custom-call(bf16[1024,3072]{1,0:T(8,128)(2,1)} %tok_hbm.1, bf16[4,192,1024]{2,1,0:T(8,128)(2,1)} %bitcast.21, s32[1024,1]{1,0:T(8,128)} %broadcast_in_dim_reshape.4.requests, bf16[4,192,128]{2,1,0:T(8,128)(2,1)} %bitcast.18, bf16[2,16,512]{2,1,0:T(8,128)(2,1)} %get-tuple-element.6.fresh_k, ...), custom_call_target="tpu_custom_call" | custom-call | flops 12884901888 | bytes 16777216 | tf_op jit(solution)/shard_map/serve/pallas_call | solution.py:485
  121.3 1.0 copy.21
  122.3 0.2 reshape.19
  122.5 0.9 copy.17
